TPU v7x, 256 devices: a whole 4x4x8 slice. The times are simulated.
256 devices in a mesh: view: 64 (over x, z, core), pix: 4 (over y).
Axes of the slice: x: 4, y: 4, z: 8, core: 2. Of those that a mesh axis runs over, the one named last changes fastest.
Arguments:
- target_tokens: bfloat16 [32768, 1024], P(('view', 'pix')), may hold values from -6 to 6
- input_tokens: bfloat16 [32768, 1024], P(('view', 'pix')), may hold values from -6 to 6
- w_query: bfloat16 [1024, 1024], P(None, 'pix')
- w_key: bfloat16 [1024, 1024], P(None, 'pix'), may hold values from -0.1875 to 0.1875
- w_value: bfloat16 [1024, 1024], P(None, 'pix'), may hold values from -0.1875 to 0.1875
- w_out: bfloat16 [1024, 1024], P('pix'), may hold values from -0.75 to 0.75
- table: int32 [256, 8], replicated, may hold values from 0 to 63, all different within a row; in each aligned block of 4 rows (0 to 3, 4 to 7, ...) at most 2 rows name the same one
- table_block: int32 [256, 8], replicated, may hold values from 0 to 3
- counts: int32 [256], P('view'), may hold values from 1 to 8
Outputs:
- output: bfloat16 [32768, 1024], P(('view', 'pix'))
Inputs may be any that keep to these rules, and one draw needn't show every extreme that they name: `table`: the entries of one row name different input views; within the rows of one target view (aligned blocks of 4 rows) no input view is named by more than 2 entries, counting all 8 columns.
All inputs are finite; a program needn't handle non-finite values.
Results may differ from a plain program's by a relative error of at most 0.0095.
The roundings to bfloat16 on the way count: a program that leaves them out, or rounds other values in their place, can miss the bound.
Values may be sent and summed in bfloat16 or wider, within the bound.
A program may use at most 128 MiB of HBM per device.

v0:
```python
import jax
import jax.numpy as jnp
from jax import lax
from jax.experimental import pallas as pl
from jax.experimental.pallas import tpu as pltpu
from jax.sharding import Mesh, PartitionSpec as P

D = 1024
HEAD_DIM = 64
BLOCK = 128
LIST_LEN = 8
PIX = 4
HALVES = 2
STRIDE = 11
HALF_ROWS = BLOCK // HALVES
CHUNK = 256
LOG2E = 1.4426950408889634


def normalize(tokens):
    source = tokens.astype(jnp.float32)
    center = source - jnp.mean(source, axis=1, keepdims=True)
    spread = jnp.mean(center * center, axis=1, keepdims=True)
    return (center * lax.rsqrt(spread + 1e-05)).astype(jnp.bfloat16)


def mod(value, power):
    return value % power if isinstance(value, int) else value & (power - 1)


def over(value, power):
    return value // power if isinstance(value, int) else value >> (power.bit_length() - 1)


def kernel(
    table_ref, block_ref, counts_ref, target_ref, tokens_ref, wq_ref, wk_ref, wv_ref, wo_ref,
    result_ref,
    listed, wq, wk, wv, wo, target, tokens, pieces, held, held_b, outgoing,
    split, values, scores, probs, peaks, sums, total, views, blocks,
    pre_send, pre_recv, ring_send, ring_recv, out_send, out_recv,
    row_send, row_recv, col_send, col_recv, slab_send, slab_recv, pair_send, pair_recv, own_sem,
):
    x, z, core, y = (lax.axis_index(name) for name in ("x", "z", "core", "pix"))
    nx, nz, nc, ny = (lax.axis_size(name) for name in ("x", "z", "core", "pix"))
    part = nc * ny
    members = nx * part
    places = (x * part + core * ny + y, z * ny + y)

    def member(half, t):
        if half == 0:
            return (over(t, part), z, mod(over(t, ny), nc), mod(t, ny))
        return (x, over(t, ny), core, mod(t, ny))

    up_z, down_z = (x, mod(z + 1, nz), core, y), (x, mod(z + nz - 1, nz), core, y)
    up_y, down_y = (x, z, core, mod(y + 1, ny)), (x, z, core, mod(y + ny - 1, ny))
    up_x, down_x = (mod(x + 1, nx), z, core, y), (mod(x + nx - 1, nx), z, core, y)
    other = (x, z, 1 - core, y)

    def remote(src, dst, send, recv, device):
        return pltpu.make_async_remote_copy(
            src_ref=src, dst_ref=dst, send_sem=send, recv_sem=recv,
            device_id=device, device_id_type=pl.DeviceIdType.MESH,
        )

    fetch = pltpu.make_async_copy(tokens_ref, tokens, own_sem.at[0])
    fetch.start()
    barrier = pltpu.get_barrier_semaphore()

    def greet(k, carry):
        for half in range(HALVES):
            pl.semaphore_signal(
                barrier, inc=1, device_id=member(half, mod(places[half] + k, members)),
                device_id_type=pl.DeviceIdType.MESH,
            )
        return carry

    for k in range(1, members):
        greet(k, 0)
    lists = [
        pltpu.make_async_copy(src, dst, own_sem.at[1 + i])
        for i, (src, dst) in enumerate(((table_ref, views), (block_ref, blocks)))
    ]
    mine = [
        pltpu.make_async_copy(src, dst, own_sem.at[3 + i])
        for i, (src, dst) in enumerate(
            ((wq_ref, wq.at[ny - 1]), (wk_ref, wk.at[ny - 1]), (wv_ref, wv.at[ny - 1]), (wo_ref, wo.at[ny - 1]), (target_ref, target))
        )
    ]
    for copy in lists + mine:
        copy.start()
    fetch.wait()
    normed = normalize(tokens[...])
    for t in range(members):
        for half in range(HALVES):
            top, left = half * HALF_ROWS + (over(t, part)) * 16, (mod(t, part)) * 128
            pieces[t, half] = normed[top:top + 16, left:left + 128]
    held[x, z * part + core * ny + y] = pieces[places[0], 0]
    held_b[x * nc + core, places[1]] = pieces[places[1], 1]
    pl.semaphore_wait(barrier, HALVES * (members - 1))

    def pre(half, t, s):
        dst = held.at[over(s, part), z * part + mod(s, part)] if half == 0 else held_b.at[x * nc + core, s]
        i = half * members
        return remote(pieces.at[t, half], dst, pre_send.at[i + t], pre_recv.at[i + s], member(half, t))

    def pre_start(k, carry):
        for half in (1, 0):
            pre(half, mod(places[half] + k, members), places[half]).start()
        return carry

    for k in range(1, members):
        pre_start(k, 0)

    class Ring:
        def __init__(self, own, slot, at, up, down, send, recv, base):
            self.own, self.slot, self.at, self.up, self.down = own, slot, at, up, down
            self.send, self.recv, self.base = send, recv, base

        def copy(self, i, src, origin, rel, half, device):
            dst = self.slot(mod(origin, 4), rel, half)
            return remote(
                dst if src is None else src, dst, self.send.at[self.base + i], self.recv.at[self.base + i], device
            )

        def begin(self):
            for half in (0, 1):
                self.copy(half, self.own(half), self.at, 3, half, self.up).start()
                self.copy(3 + half, self.own(half), self.at, 1, half, self.down).start()

        def forward(self):
            before, after = mod(self.at + 3, 4), mod(self.at + 1, 4)
            self.copy(0, None, before, 3, 0, self.up).wait_recv()
            self.copy(2, self.slot(before, 3, 0), before, 2, 0, self.up).start()
            self.copy(4, None, after, 1, 1, self.down).wait_recv()
            self.copy(5, self.slot(after, 1, 1), after, 2, 1, self.down).start()

        def end(self):
            self.copy(1, None, self.at + 3, 3, 1, self.up).wait_recv()
            self.copy(3, None, self.at + 1, 1, 0, self.down).wait_recv()
            self.copy(2, None, self.at + 2, 2, 0, self.up).wait_recv()
            self.copy(5, None, self.at + 2, 2, 1, self.down).wait_recv()

        def sent(self):
            for i in range(6):
                self.copy(i, None, self.at + 2, 2, (0, 1, 0, 0, 1, 1)[i], self.up).wait_send()

    def y_ring(src, dst, start, size, base):
        return Ring(
            lambda half: src.at[pl.ds(start + half * size, size)],
            lambda origin, rel, half: dst.at[rel - 1, pl.ds(start + half * size, size)],
            y, up_y, down_y, row_send, row_recv, base,
        )

    def x_ring(dst, size, base):
        def slot(origin, rel, half):
            start = core * 8 * size + origin * 2 * size + half * size
            return dst.at[pl.ds(0, 3), pl.ds(pl.multiple_of(start, size), size)]

        return Ring(lambda half: slot(x, 0, half), slot, x, up_x, down_x, col_send, col_recv, base)

    narrow = [
        y_ring(src, dst, pl.multiple_of((core * nx + x) * 2 * size, 2 * size), size, 6 * i)
        for i, (src, dst, size) in enumerate(((wq_ref, wq, 64), (wv_ref, wv, 64), (wo_ref, wo, 16)))
    ]
    wide = y_ring(wk_ref, wk, pl.multiple_of(core * 512, 512), 256, 18)
    across = [x_ring(dst, size, 6 * i) for i, (dst, size) in enumerate(((wq, 64), (wv, 64), (wo, 16)))]

    def slab_slot(origin, rel, half):
        return held_b.at[origin * nc + core, pl.ds(half * 16, 16)]

    beside = Ring(lambda half: slab_slot(x, 0, half), slab_slot, x, up_x, down_x, col_send, col_recv, 18)

    def slab(origin, side):
        ref = held_b.at[origin * nc + side]
        return remote(ref, ref, slab_send.at[origin], slab_recv.at[origin], other)

    def pair(kind, side):
        dst, rows = ((wq, 512), (wk, 512), (wv, 512), (wo, 128))[kind]
        ref = dst.at[pl.ds(0, 3), pl.ds(pl.multiple_of(side * rows, rows), rows)]
        return remote(ref, ref, pair_send.at[kind], pair_recv.at[kind], other)

    for ring in (*narrow, wide):
        ring.begin()

    def turn(q):
        return mod(x + nx - q, nx)

    def hop(way, distance, q, origin):
        ref = held.at[turn(q), pl.ds(pl.multiple_of(origin * part, part), part)]
        i = (way * 4 + distance - 1) * nx + q
        return remote(ref, ref, ring_send.at[i], ring_recv.at[i], (up_z, down_z)[way])

    def origin_of(way, distance):
        return mod(z + nz - distance, nz) if way == 0 else mod(z + distance, nz)

    def goes(way, distance, q):
        return distance < 4 or (q < nx // 2) == (way == 0)

    def ring_begin(q):
        for way in (0, 1):
            hop(way, 1, q, z).start()

    def ring_step(distance):
        for q in range(nx):
            for way in (0, 1):
                if goes(way, distance, q):
                    hop(way, distance, q, origin_of(way, distance)).wait_recv()
                    if distance < 4 and goes(way, distance + 1, q):
                        hop(way, distance + 1, q, origin_of(way, distance)).start()

    def spot(half, s):
        return listed.at[
            half, :,
            pl.ds(pl.multiple_of((over(s, part)) * 16, 16), 16),
            pl.ds(pl.multiple_of((mod(s, part)) * 128, 128), 128),
        ]

    def out(half, t, s):
        i = half * members
        return remote(
            outgoing.at[half, t], spot(half, s), out_send.at[i + t], out_recv.at[i + s], member(half, t)
        )

    def pick(half, t):
        row = (over(t, part) * nz + z) * part + mod(t, part) if half == 0 else (x * nz + over(t, ny)) * part + core * ny + mod(t, ny)
        for e in range(LIST_LEN):
            view, block = views[e, row], blocks[e, row]
            if half == 0:
                outgoing[half, t, e] = held[over(view, 16), mod(view, 16) * ny + block]
            else:
                outgoing[half, t, e] = held_b[over(view, 16) * nc + mod(view, 2), over(mod(view, 16), 2) * ny + block]

    def deal(half, first, last):
        me = places[half]

        def start(k, carry):
            t = mod(me + k * STRIDE, members)
            pick(half, t)
            out(half, t, me).start()
            return carry

        lax.fori_loop(first, last, start, 0)

    def keep(half):
        me = places[half]
        pick(half, me)
        copy = pltpu.make_async_copy(outgoing.at[half, me], spot(half, me), own_sem.at[9 + half])
        copy.start()
        return copy

    def pre_wait(half, first, last):
        def wait(s, carry):
            @pl.when(s != places[half])
            def _():
                pre(half, s, s).wait_recv()
            return carry

        lax.fori_loop(first, last, wait, 0)

    pre_wait(1, 0, members)
    beside.begin()
    slab(x, core).start()
    for q in range(nx):
        pre_wait(0, turn(q) * part, turn(q) * part + part)
        ring_begin(q)
    for copy in lists:
        copy.wait()

    beside.forward()
    ring_step(1)
    for ring in narrow:
        ring.forward()
    beside.end()
    for i in range(1, nx):
        slab(mod(x + i, nx), core).start()
    ring_step(2)
    wide.forward()
    for ring, far in zip(narrow, across):
        ring.end()
        far.begin()
    for i in range(nx):
        slab(mod(x + i, nx), 1 - core).wait_recv()
    deal(1, 1, 16)
    ring_step(3)
    deal(1, 16, members)
    late = keep(1)
    for ring in across:
        ring.forward()
    ring_step(4)
    wide.end()
    pair(1, core).start()
    deal(0, 1, 16)
    for kind, ring in zip((0, 2), across):
        ring.end()
        pair(kind, core).start()
    deal(0, 16, members)
    local = [keep(0), late]
    across[2].end()
    pair(3, core).start()

    for copy in mine:
        copy.wait()
    pair(0, 1 - core).wait_recv()
    wide_cols = D // ny
    group_heads = wide_cols // HEAD_DIM
    lane_head = over(lax.broadcasted_iota(jnp.int32, (1, wide_cols), 1), HEAD_DIM)
    aim = normalize(target[...])
    for g in range(ny):
        query = jnp.dot(aim, wq[g], preferred_element_type=jnp.float32)
        for h in range(group_heads):
            split[g, h * BLOCK:(h + 1) * BLOCK] = jnp.where(lane_head == h, query, 0.0).astype(jnp.bfloat16)
    for kind in (1, 2):
        pair(kind, 1 - core).wait_recv()

    span = LIST_LEN * HALF_ROWS
    columns = lax.broadcasted_iota(jnp.int32, (1, span), 1)
    shade = jnp.where(columns < counts_ref[y] * HALF_ROWS, 0.0, -1e30)
    stretch = HEAD_DIM ** (-0.5) * LOG2E

    def arrive(half):
        def wait(k, carry):
            s = mod(places[half] + k, members)
            out(half, s, s).wait_recv()
            return carry

        lax.fori_loop(1, members, wait, 0)
        local[half].wait()

    def project(half):
        rows = listed[half].reshape(span, D)
        at = slice(half * span, (half + 1) * span)
        for g in range(ny):
            key = jnp.dot(rows, wk[g], preferred_element_type=jnp.float32).astype(jnp.bfloat16)
            values[g, at] = jnp.dot(rows, wv[g], preferred_element_type=jnp.float32).astype(jnp.bfloat16)
            scores[g, :, at] = lax.dot_general(
                split[g], key, (((1,), (1,)), ((), ())), preferred_element_type=jnp.float32
            )

    per_group = group_heads * BLOCK // CHUNK

    def chunk_at(i):
        return over(i, per_group), pl.ds(pl.multiple_of(mod(i, per_group) * CHUNK, CHUNK), CHUNK)

    def soften(i, carry):
        g, rows = chunk_at(i)
        logits = scores[g, rows, span:2 * span] + shade
        peak = jnp.max(logits, axis=1, keepdims=True)
        weights = jnp.exp2((logits - peak) * stretch)
        scores[g, rows, span:2 * span] = weights
        peaks[g, rows] = jnp.broadcast_to(peak, (CHUNK, 128))
        sums[g, rows] = jnp.broadcast_to(jnp.sum(weights, axis=1, keepdims=True), (CHUNK, 128))
        return carry

    def finish(g, rows):
        logits = scores[g, rows, 0:span] + shade
        before = peaks[g, rows][:, 0:1]
        peak = jnp.maximum(before, jnp.max(logits, axis=1, keepdims=True))
        weights = jnp.exp2((logits - peak) * stretch)
        fade = jnp.exp2((before - peak) * stretch)
        whole = fade * sums[g, rows][:, 0:1] + jnp.sum(weights, axis=1, keepdims=True)
        share = 1.0 / whole
        probs[g, rows, 0:span] = (weights * share).astype(jnp.bfloat16)
        probs[g, rows, span:2 * span] = (scores[g, rows, span:2 * span] * (fade * share)).astype(jnp.bfloat16)

    arrive(1)
    project(1)
    lax.fori_loop(0, ny * per_group, soften, 0)
    arrive(0)
    project(0)
    pair(3, 1 - core).wait_recv()
    mixed = jnp.zeros((BLOCK, D), jnp.float32)
    for g in range(ny):
        for h in range(group_heads):
            finish(g, slice(h * BLOCK, (h + 1) * BLOCK))
        summed = jnp.dot(probs[g], values[g], preferred_element_type=jnp.float32)
        attended = jnp.zeros((BLOCK, wide_cols), jnp.float32)
        for h in range(group_heads):
            attended = jnp.where(lane_head == h, summed[h * BLOCK:(h + 1) * BLOCK], attended)
        mixed += jnp.dot(attended.astype(jnp.bfloat16), wo[g], preferred_element_type=jnp.float32)
    total[...] = (target[...].astype(jnp.float32) + mixed).astype(jnp.bfloat16)
    deliver = pltpu.make_async_copy(total, result_ref, own_sem.at[8])
    deliver.start()

    def drain(k, carry):
        for half in range(HALVES):
            t = mod(places[half] + k, members)
            pre(half, t, places[half]).wait_send()
            out(half, t, places[half]).wait_send()
        return carry

    lax.fori_loop(1, members, drain, 0)
    for way in (0, 1):
        for distance in range(1, 5):
            for q in range(nx):
                if goes(way, distance, q):
                    hop(way, distance, q, z).wait_send()
    for ring in (*narrow, wide, *across, beside):
        ring.sent()
    for i in range(nx):
        slab(mod(x + i, nx), core).wait_send()
    for kind in range(4):
        pair(kind, core).wait_send()
    deliver.wait()


def body(target_tokens, input_tokens, w_query, w_key, w_value, w_out, table, table_block, counts):
    members = 32
    cols = D // PIX
    smem, hbm = pl.BlockSpec(memory_space=pltpu.SMEM), pl.BlockSpec(memory_space=pltpu.HBM)
    dma = pltpu.SemaphoreType.DMA
    tall = pltpu.VMEM((PIX, D, cols), jnp.bfloat16)
    block = pltpu.VMEM((BLOCK, D), jnp.bfloat16)
    listed_rows = LIST_LEN * BLOCK
    stats = pltpu.VMEM((PIX, 4 * BLOCK, 128), jnp.float32)
    return pl.pallas_call(
        kernel,
        out_shape=jax.ShapeDtypeStruct((BLOCK, D), jnp.bfloat16),
        in_specs=[hbm, hbm, smem] + [hbm] * 6,
        out_specs=hbm,
        scratch_shapes=[
            pltpu.VMEM((HALVES, LIST_LEN, HALF_ROWS, D), jnp.bfloat16),
            tall, tall, tall,
            pltpu.VMEM((PIX, cols, D), jnp.bfloat16),
            block, block,
            pltpu.VMEM((members, HALVES, 16, 128), jnp.bfloat16),
            pltpu.VMEM((4, 64, 16, 128), jnp.bfloat16),
            pltpu.VMEM((8, 32, 16, 128), jnp.bfloat16),
            pltpu.VMEM((HALVES, members, LIST_LEN, 16, 128), jnp.bfloat16),
            pltpu.VMEM((PIX, 4 * BLOCK, cols), jnp.bfloat16),
            pltpu.VMEM((PIX, listed_rows, cols), jnp.bfloat16),
            pltpu.VMEM((PIX, 4 * BLOCK, listed_rows), jnp.float32),
            pltpu.VMEM((PIX, 4 * BLOCK, listed_rows), jnp.bfloat16),
            stats, stats,
            block,
            pltpu.SMEM((LIST_LEN, 8 * members), jnp.int32),
            pltpu.SMEM((LIST_LEN, 8 * members), jnp.int32),
            dma((HALVES * members,)), dma((HALVES * members,)),
            dma((32,)), dma((32,)),
            dma((HALVES * members,)), dma((HALVES * members,)),
            dma((24,)), dma((24,)),
            dma((24,)), dma((24,)),
            dma((4,)), dma((4,)),
            dma((4,)), dma((4,)),
            dma((9 + HALVES,)),
        ],
        compiler_params=pltpu.CompilerParams(
            collective_id=0, has_side_effects=True, vmem_limit_bytes=60 * 1024 * 1024
        ),
        cost_estimate=pl.CostEstimate(flops=5_400_000_000, bytes_accessed=3 << 20, transcendentals=2 << 20),
    )(table.T, table_block.T, counts, target_tokens, input_tokens, w_query, w_key, w_value, w_out)


def solution(mesh):
    views = ("x", "z", "core")
    fine = Mesh(mesh.devices.reshape(4, 8, 2, 4), ("x", "z", "core", "pix"))
    placed = (
        P((*views, "pix"), None),
        P((*views, "pix"), None),
        P(None, "pix"),
        P(None, "pix"),
        P(None, "pix"),
        P("pix", None),
        P(),
        P(),
        P(views),
    )
    return jax.shard_map(
        body, mesh=fine, in_specs=placed, out_specs=P((*views, "pix"), None), check_vma=False
    )
```

profile of v0, /device:TPU:1, one launch (start us, length us, event | category | flops | bytes accessed | tf_op | source)
XLA Modules:
  0.0 76.2 jit_solution(17663334896278190784)
XLA Ops:
  0.0 74.5 %shard_map.91 = bf16[128,1024]{1,0:T(8,128)(2,1)} custom-call(s32[8,256]{1,0:T(8,128)} %bitcast.2, s32[8,256]{1,0:T(8,128)} %bitcast.3, s32[4]{0:T(128)} %counts_ref.1, bf16[128,1024]{1,0:T(8,128)(2,1)} %target_ref.1, bf16[128,1024]{1,0:T(8,128)(2,1)} %tokens_ref.1, bf16[1024,256]{1,0:T(8,128)(2,1)} %wq_ref.1, bf16[1024,256]{1,0:T(8,128)(2,1)} %wk_ref.1, ...), custom_call_target="tpu_custom_call" | custom-call | flops 5400000000 | bytes 3145728 | tf_op jit(solution)/shard_map/pallas_call | solution.py:415
  74.5 1.7 %copy.11 = bf16[128,1024]{1,0:T(8,128)(2,1)} copy(bf16[128,1024]{1,0:T(8,128)(2,1)} %shard_map.91) | data formatting | bytes 524288
where the time goes:
time: 77.3 us; the launch traced here: 76.2 us
  Pallas kernels  74.5 us (96%)
  local copies, waits for them, and re-layouts  1.67 us (2%)
    pallas_call x1, Pallas kernels, body(): pl.pallas_call(kernel, out_shape=jax.ShapeDtypeStruct((BLOCK, D), jnp.bfl...  74.5 us
    unnamed x1, local copies, waits for them, and re-layouts  1.67 us

commit v1 on v0

--- a/solution.py
+++ b/solution.py
@@ -234,7 +234,12 @@
         me = places[half]
 
         def start(k, carry):
-            t = mod(me + k * STRIDE, members)
+            if half == 1:
+                t = mod(me + k * STRIDE, members)
+            elif last < members:
+                t = mod(me + 24 + mod(8 + 5 * k, 16), members)
+            else:
+                t = mod(me + 8 + mod(5 * k, 16), members)
             pick(half, t)
             out(half, t, me).start()
             return carry
@@ -315,6 +320,7 @@
     span = LIST_LEN * HALF_ROWS
     columns = lax.broadcasted_iota(jnp.int32, (1, span), 1)
     shade = jnp.where(columns < counts_ref[y] * HALF_ROWS, 0.0, -1e30)
+    fine_shade = jnp.where(mod(columns, LIST_LEN * 16) < counts_ref[y] * 16, 0.0, -1e30)
     stretch = HEAD_DIM ** (-0.5) * LOG2E
 
     def arrive(half):
@@ -326,9 +332,7 @@
         lax.fori_loop(1, members, wait, 0)
         local[half].wait()
 
-    def project(half):
-        rows = listed[half].reshape(span, D)
-        at = slice(half * span, (half + 1) * span)
+    def absorb(rows, at):
         for g in range(ny):
             key = jnp.dot(rows, wk[g], preferred_element_type=jnp.float32).astype(jnp.bfloat16)
             values[g, at] = jnp.dot(rows, wv[g], preferred_element_type=jnp.float32).astype(jnp.bfloat16)
@@ -352,7 +356,7 @@
         return carry
 
     def finish(g, rows):
-        logits = scores[g, rows, 0:span] + shade
+        logits = scores[g, rows, 0:span] + fine_shade
         before = peaks[g, rows][:, 0:1]
         peak = jnp.maximum(before, jnp.max(logits, axis=1, keepdims=True))
         weights = jnp.exp2((logits - peak) * stretch)
@@ -363,10 +367,29 @@
         probs[g, rows, span:2 * span] = (scores[g, rows, span:2 * span] * (fade * share)).astype(jnp.bfloat16)
 
     arrive(1)
-    project(1)
+    absorb(listed[1].reshape(span, D), slice(span, 2 * span))
     lax.fori_loop(0, ny * per_group, soften, 0)
-    arrive(0)
-    project(0)
+    for late in range(2):
+        for i in (2 * late, 2 * late + 1):
+            first = mod(x + i, nx) * part
+
+            def wait(s, carry):
+                @pl.when(s != places[0])
+                def _():
+                    out(0, s, s).wait_recv()
+                return carry
+
+            lax.fori_loop(first, first + part, wait, 0)
+        if late == 0:
+            local[0].wait()
+        rows = jnp.concatenate(
+            [
+                listed[0, :, pl.ds(pl.multiple_of(mod(x + i, nx) * 16, 16), 16)].reshape(LIST_LEN * 16, D)
+                for i in (2 * late, 2 * late + 1)
+            ],
+            axis=0,
+        )
+        absorb(rows, slice(late * span // 2, (late + 1) * span // 2))
     pair(3, 1 - core).wait_recv()
     mixed = jnp.zeros((BLOCK, D), jnp.float32)
     for g in range(ny):

time: 77.3 us -> 77.5 us (level)
  no operation moved by 1% of the time
where the time goes in v1:
time: 77.5 us; the launch traced here: 76.8 us
  Pallas kernels  75.1 us (97%)
  local copies, waits for them, and re-layouts  1.67 us (2%)
    pallas_call x1, Pallas kernels, body(): pl.pallas_call(kernel, out_shape=jax.ShapeDtypeStruct((BLOCK, D), jnp.bfl...  75.1 us
    unnamed x1, local copies, waits for them, and re-layouts  1.67 us

profile of v1, /device:TPU:1, one launch (start us, length us, event | category | flops | bytes accessed | tf_op | source)
XLA Modules:
  0.0 76.8 jit_solution(3827128817097954871)
XLA Ops:
  0.0 75.1 %shard_map.91 = bf16[128,1024]{1,0:T(8,128)(2,1)} custom-call(s32[8,256]{1,0:T(8,128)} %bitcast.2, s32[8,256]{1,0:T(8,128)} %bitcast.3, s32[4]{0:T(128)} %counts_ref.1, bf16[128,1024]{1,0:T(8,128)(2,1)} %target_ref.1, bf16[128,1024]{1,0:T(8,128)(2,1)} %tokens_ref.1, bf16[1024,256]{1,0:T(8,128)(2,1)} %wq_ref.1, bf16[1024,256]{1,0:T(8,128)(2,1)} %wk_ref.1, ...), custom_call_target="tpu_custom_call" | custom-call | flops 5400000000 | bytes 3145728 | tf_op jit(solution)/shard_map/pallas_call | solution.py:438
  75.1 1.7 %copy.11 = bf16[128,1024]{1,0:T(8,128)(2,1)} copy(bf16[128,1024]{1,0:T(8,128)(2,1)} %shard_map.91) | data formatting | bytes 524288
